TPU v7x, 512 devices: a whole 4x4x16 slice. The times are simulated.
512 devices in a mesh: grp: 16 (over y, x), tile: 32 (over z, core).
Axes of the slice: x: 4, y: 4, z: 16, core: 2. Of those that a mesh axis runs over, the one named last changes fastest.
Arguments:
- latent: bfloat16 [8, 64, 64, 512], P(None, 'grp', 'tile'), may hold values from -36 to 36
- coarse_filters: bfloat16 [3, 3, 3, 512, 512], P(None, None, None, None, 'grp'), may hold values from -0.0546875 to 0.0546875
- mid_filters: bfloat16 [3, 3, 3, 256, 256], P(None, None, None, None, 'tile'), may hold values from -0.078125 to 0.078125
- fine_filters: bfloat16 [3, 3, 3, 128, 128], replicated, may hold values from -0.109375 to 0.109375
- coarse_proj: bfloat16 [512, 256], replicated, may hold values from -0.25 to 0.25
- mid_proj: bfloat16 [256, 128], replicated, may hold values from -0.375 to 0.375
Outputs:
- frames_out: bfloat16 [8, 256, 256, 128], P(None, 'grp', 'tile')
All inputs are finite; a program needn't handle non-finite values.
Results may differ from a plain program's by a relative error of at most 0.018.
Values may be sent and summed in bfloat16 or wider, within the bound.
A program may use at most 128 MiB of HBM per device.

v0:
```python
import jax
import jax.numpy as jnp
from jax import lax
from jax.sharding import PartitionSpec as P


def with_halo(shard, sides, width):
    for axis, dim in sides:
        size, length = (lax.axis_size(axis), shard.shape[dim])
        up = [(i, (i + 1) % size) for i in range(size - 1)]
        down = [(j, i) for i, j in up]
        last = lax.slice_in_dim(shard, length - width, length, axis=dim)
        initial = lax.slice_in_dim(shard, 0, width, axis=dim)
        before = lax.ppermute(last, axis, up)
        after = lax.ppermute(initial, axis, down)
        shard = jnp.concatenate([before, shard, after], axis=dim)
    return shard


def activate(values):
    widened = values.astype(jnp.float32)
    scaled = widened * lax.rsqrt(jnp.mean(widened * widened, axis=-1, keepdims=True) + 1e-06)
    return jax.nn.silu(scaled).astype(jnp.bfloat16)


def double_size(values):
    return jnp.repeat(jnp.repeat(values, 2, axis=1), 2, axis=2)


def time_padded(values):
    return jnp.pad(values, ((2, 0), (0, 0), (0, 0), (0, 0)))


def stencil_columns(extended):
    padded = time_padded(extended)
    height = extended.shape[1] - 2
    breadth = extended.shape[2] - 2
    return jnp.concatenate(
        [
            padded[:, row_step : row_step + height, col_step : col_step + breadth, :]
            for row_step in range(3)
            for col_step in range(3)
        ],
        axis=-1,
    )


def apply_columns(columns, filters):
    frames = columns.shape[0] - 2
    folded = filters.reshape(3, 9 * filters.shape[3], filters.shape[4])
    total = jnp.dot(columns[0:frames], folded[0], preferred_element_type=jnp.float32)
    for frame_step in (1, 2):
        total = total + jnp.dot(
            columns[frame_step : frame_step + frames],
            folded[frame_step],
            preferred_element_type=jnp.float32,
        )
    return total


def coarse_conv(extended, filters):
    padded = time_padded(extended)
    frames = extended.shape[0]
    height = extended.shape[1] - 2
    breadth = extended.shape[2] - 2
    inputs = filters.shape[3]
    outputs = filters.shape[4]
    total = jnp.zeros((frames, height, breadth, outputs), jnp.float32)
    for frame_step in range(3):
        spread = jnp.transpose(filters[frame_step], (2, 0, 1, 3)).reshape(inputs, 9 * outputs)
        products = jnp.dot(
            padded[frame_step : frame_step + frames], spread, preferred_element_type=jnp.float32
        )
        for row_step in range(3):
            for col_step in range(3):
                lane = 3 * row_step + col_step
                total = (
                    total
                    + products[
                        :,
                        row_step : row_step + height,
                        col_step : col_step + breadth,
                        lane * outputs : (lane + 1) * outputs,
                    ]
                )
    return total


def middle_conv(extended, mid_filters):
    columns = stencil_columns(extended)
    return apply_columns(columns, lax.all_gather(mid_filters, "tile", axis=4, tiled=True))


def body(latent, coarse_filters, mid_filters, fine_filters, coarse_proj, mid_proj):
    first_act = activate(latent)
    whole = lax.all_gather(first_act, "grp", axis=1, tiled=True)
    widened = with_halo(whole, (("tile", 2),), 1)
    padded = jnp.pad(widened, ((0, 0), (1, 1), (0, 0), (0, 0)))
    filtered = coarse_conv(padded, coarse_filters).astype(jnp.bfloat16)
    returned = lax.all_to_all(filtered, "grp", split_axis=1, concat_axis=3, tiled=True)
    level_zero = (latent.astype(jnp.float32) + returned.astype(jnp.float32)).astype(jnp.bfloat16)
    reduced = jnp.dot(level_zero, coarse_proj, preferred_element_type=jnp.float32).astype(
        jnp.bfloat16
    )
    mid_act = double_size(activate(reduced))
    mid_ext = with_halo(mid_act, (("grp", 1), ("tile", 2)), 1)
    mid_terms = middle_conv(mid_ext, mid_filters)
    mid_out = (double_size(reduced).astype(jnp.float32) + mid_terms).astype(jnp.bfloat16)
    fine_low = jnp.dot(mid_out, mid_proj, preferred_element_type=jnp.float32).astype(jnp.bfloat16)
    fine_in = double_size(fine_low)
    fine_act = double_size(activate(fine_low))
    fine_ext = with_halo(fine_act, (("grp", 1), ("tile", 2)), 1)
    fine_terms = apply_columns(stencil_columns(fine_ext), fine_filters)
    return (fine_in.astype(jnp.float32) + fine_terms).astype(jnp.bfloat16)


def solution(mesh):
    in_specs = (
        P(None, "grp", "tile", None),
        P(None, None, None, None, "grp"),
        P(None, None, None, None, "tile"),
        P(),
        P(),
        P(),
    )
    out_specs = P(None, "grp", "tile", None)
    return jax.shard_map(body, mesh=mesh, in_specs=in_specs, out_specs=out_specs, check_vma=False)
```

profile of v0, /device:TPU:7, one launch (start us, length us, event | category | flops | bytes accessed | tf_op | source)
XLA Modules:
  0.0 200.4 jit_solution(11646952750403236550)
XLA Ops:
  10.0 61.1 %all-gather.3.cloned.1.call-done = bf16[8,64,2,512]{3,0,2,1:T(8,128)(2,1)} async-done(((bf16[8,4,2,512]{3,0,2,1:T(8,128)(2,1)}), bf16[8,64,2,512]{3,0,2,1:T(8,128)(2,1)}) %all-gather.3.cloned.1.call-update) | async-done | bytes 1048592 | tf_op jit(solution)/shard_map/all_gather | solution.py:96
  73.0 5.1 %collective-permute-start = (bf16[8,64,1,512]{3,1,2,0:T(8,128)(2,1)S(1)}, bf16[8,64,1,512]{3,1,2,0:T(8,128)(2,1)S(1)}, u32[]{:S(2)}, u32[]{:S(2)}) collective-permute-start(bf16[8,64,1,512]{3,1,2,0:T(8,128)(2,1)S(1)} %get-tuple-element.8), channel_id=1, source_target_pairs={{0,1},{1,2},{2,3},{3,4},{4,5},{5,6},{6,7},{7,8},{8,9},{9,10},{10,1... | collective-permute-start | bytes 1572872 | tf_op jit(solution)/shard_map/ppermute | solution.py:14
  80.0 4.1 %collective-permute-done = bf16[8,64,1,512]{3,1,2,0:T(8,128)(2,1)S(1)} collective-permute-done((bf16[8,64,1,512]{3,1,2,0:T(8,128)(2,1)S(1)}, bf16[8,64,1,512]{3,1,2,0:T(8,128)(2,1)S(1)}, u32[]{:S(2)}, u32[]{:S(2)}) %collective-permute-start) | collective-permute-done | bytes 524320 | tf_op jit(solution)/shard_map/ppermute | solution.py:14
  84.1 4.4 %collective-permute-done.1 = bf16[8,64,1,512]{3,1,2,0:T(8,128)(2,1)S(1)} collective-permute-done((bf16[8,64,1,512]{3,1,2,0:T(8,128)(2,1)S(1)}, bf16[8,64,1,512]{3,1,2,0:T(8,128)(2,1)S(1)}, u32[]{:S(2)}, u32[]{:S(2)}) %collective-permute-start.1) | collective-permute-done | bytes 524320 | tf_op jit(solution)/shard_map/ppermute | solution.py:15
  93.9 2.5 %fusion.24 = bf16[8,64,2,32]{3,1,2,0:T(8,128)(2,1)S(1)} fusion(f32[8,66,4,288]{3,1,2,0:T(8,128)S(1)} %fusion.47, f32[8,66,4,288]{3,1,2,0:T(8,128)S(1)} %fusion.51, f32[8,66,4,288]{3,1,2,0:T(8,128)S(1)} %fusion.50), kind=kLoop, calls=%fused_computation.35 | loop fusion | flops 884736 | bytes 3604480 | tf_op jit(solution)/shard_map/convert_element_type | solution.py:99
  97.0 9.8 %all_to_all.4 = bf16[16,2,1024]{2,1,0:T(2,128)(2,1)S(1)} all-to-all(bf16[16,2,1024]{2,1,0:T(2,128)(2,1)S(1)} %reshape.91), channel_id=1, replica_groups=mesh['grp'=16,'tile'=32] {'grp'}, dimensions={0} | all-to-all | bytes 131072 | tf_op jit(solution)/shard_map/all_to_all | solution.py:100
  108.0 3.7 %collective-permute-start.2 = (bf16[8,1,4,256]{3,2,1,0:T(4,128)(2,1)S(1)}, bf16[8,1,4,256]{3,2,1,0:T(4,128)(2,1)S(1)}, u32[]{:S(2)}, u32[]{:S(2)}) collective-permute-start(bf16[8,1,4,256]{3,2,1,0:T(4,128)(2,1)S(1)} %get-tuple-element.23), channel_id=1, source_target_pairs={{0,32},{32,64},{64,96},{96,128},{128,160},{160,192},{192,224},{224... | collective-permute-start | bytes 49160 | tf_op jit(solution)/shard_map/ppermute | solution.py:14
  111.7 1.9 collective-permute-start.3
  113.7 4.6 %collective-permute-done.3 = bf16[8,1,4,256]{3,2,1,0:T(4,128)(2,1)S(1)} collective-permute-done((bf16[8,1,4,256]{3,2,1,0:T(4,128)(2,1)S(1)}, bf16[8,1,4,256]{3,2,1,0:T(4,128)(2,1)S(1)}, u32[]{:S(2)}, u32[]{:S(2)}) %collective-permute-start.3) | collective-permute-done | bytes 16416 | tf_op jit(solution)/shard_map/ppermute | solution.py:15
  118.4 4.6 %collective-permute-start.4 = (bf16[8,10,1,256]{3,2,1,0:T(2,128)(2,1)S(1)}, bf16[8,10,1,256]{3,2,1,0:T(2,128)(2,1)S(1)}, u32[]{:S(2)}, u32[]{:S(2)}) collective-permute-start(bf16[8,10,1,256]{3,2,1,0:T(2,128)(2,1)S(1)} %get-tuple-element.20), channel_id=1, source_target_pairs={{0,1},{1,2},{2,3},{3,4},{4,5},{5,6},{6,7},{7,8},{8,9},{9,10},{10,1... | collective-permute-start | bytes 122888 | tf_op jit(solution)/shard_map/ppermute | solution.py:14
  123.1 2.1 %collective-permute-start.5 = (bf16[8,10,1,256]{3,2,1,0:T(2,128)(2,1)S(1)}, bf16[8,10,1,256]{3,2,1,0:T(2,128)(2,1)S(1)}, u32[]{:S(2)}, u32[]{:S(2)}) collective-permute-start(bf16[8,10,1,256]{3,2,1,0:T(2,128)(2,1)S(1)} %get-tuple-element.21), channel_id=1, source_target_pairs={{1,0},{2,1},{3,2},{4,3},{5,4},{6,5},{7,6},{8,7},{9,8},{10,9},{11,1... | collective-permute-start | bytes 122888 | tf_op jit(solution)/shard_map/ppermute | solution.py:15
  125.6 3.7 %collective-permute-done.5 = bf16[8,10,1,256]{3,2,1,0:T(2,128)(2,1)S(1)} collective-permute-done((bf16[8,10,1,256]{3,2,1,0:T(2,128)(2,1)S(1)}, bf16[8,10,1,256]{3,2,1,0:T(2,128)(2,1)S(1)}, u32[]{:S(2)}, u32[]{:S(2)}) %collective-permute-start.5) | collective-permute-done | bytes 40992 | tf_op jit(solution)/shard_map/ppermute | solution.py:15
  136.8 16.2 %all-gather.5.cloned.1.call-done = bf16[3,3,3,256,256]{3,4,2,1,0:T(8,128)(2,1)} async-done(((bf16[3,3,3,256,8]{3,4,2,1,0:T(8,128)(2,1)}), bf16[3,3,3,256,256]{3,4,2,1,0:T(8,128)(2,1)}) %all-gather.5.cloned.1.call-update) | async-done | bytes 3538960 | tf_op jit(solution)/shard_map/all_gather | solution.py:91
  153.0 3.3 %fusion.40 = (bf16[1,3,3,256,256]{3,4,2,1,0:T(8,128)(2,1)S(1)}, bf16[1,3,3,256,256]{3,4,2,1,0:T(8,128)(2,1)S(1)}, bf16[1,3,3,256,256]{3,4,2,1,0:T(8,128)(2,1)}) fusion(bf16[3,3,3,256,256]{3,4,2,1,0:T(8,128)(2,1)} %all-gather.5.cloned.1.call-done), kind=kLoop, calls=%fused_computation.110 | loop fusion | bytes 7077888 | tf_op jit(solution)/shard_map/slice | solution.py:55
  156.3 2.4 %copy.49 = bf16[1,3,3,256,256]{4,3,2,1,0:T(8,128)(2,1)} copy(bf16[1,3,3,256,256]{3,4,2,1,0:T(8,128)(2,1)} %get-tuple-element.7) | data formatting | bytes 2359296
  161.0 2.4 %fusion.48 = f32[8,8,4,256]{3,2,1,0:T(4,128)S(1)} fusion(bf16[10,8,4,2304]{3,2,1,0:T(4,128)(2,1)} %slice_dynamic-update-slice_fusion.9, bf16[2304,256,1,1]{1,0,3,2:T(8,128)(2,1)} %bitcast.115), kind=kOutput, calls=%fused_computation.119 | convolution fusion | flops 301989888 | bytes 2916352 | tf_op jit(solution)/shard_map/dot_general | solution.py:51
  163.4 2.0 convolution_add_fusion.3
  165.4 2.1 %fusion.14 = bf16[8,8,4,256]{3,2,1,0:T(4,128)(2,1)S(1)} fusion(f32[8,8,4,256]{3,2,1,0:T(4,128)S(1)} %convert_element_type.86, f32[8,8,4,256]{3,2,1,0:T(4,128)S(1)} %convolution_add_fusion.3, bf16[10,8,4,2304]{3,2,1,0:T(4,128)(2,1)} %slice_dynamic-update-slice_fusion.9, bf16[2304,256,1,1]{1,0,3,2:T(8,128)(2,1)S(1)} %bitcast.114), kind=kOutput, calls=%fused_computation.21 | convolution fusion | flops 302186496 | bytes 3309568 | tf_op jit(solution)/shard_map/dot_general | solution.py:53
  168.2 2.7 %collective-permute-start.6 = (bf16[8,1,8,128]{3,2,1,0:T(8,128)(2,1)S(1)}, bf16[8,1,8,128]{3,2,1,0:T(8,128)(2,1)S(1)}, u32[]{:S(2)}, u32[]{:S(2)}) collective-permute-start(bf16[8,1,8,128]{3,2,1,0:T(8,128)(2,1)S(1)} %get-tuple-element.18), channel_id=1, source_target_pairs={{0,32},{32,64},{64,96},{96,128},{128,160},{160,192},{192,224},{224... | collective-permute-start | bytes 49160 | tf_op jit(solution)/shard_map/ppermute | solution.py:14
  170.9 2.6 %collective-permute-start.7 = (bf16[8,1,8,128]{3,2,1,0:T(8,128)(2,1)S(1)}, bf16[8,1,8,128]{3,2,1,0:T(8,128)(2,1)S(1)}, u32[]{:S(2)}, u32[]{:S(2)}) collective-permute-start(bf16[8,1,8,128]{3,2,1,0:T(8,128)(2,1)S(1)} %get-tuple-element.19), channel_id=1, source_target_pairs={{32,0},{64,32},{96,64},{128,96},{160,128},{192,160},{224,192},{256... | collective-permute-start | bytes 49160 | tf_op jit(solution)/shard_map/ppermute | solution.py:15
  173.5 4.0 %collective-permute-done.7 = bf16[8,1,8,128]{3,2,1,0:T(8,128)(2,1)S(1)} collective-permute-done((bf16[8,1,8,128]{3,2,1,0:T(8,128)(2,1)S(1)}, bf16[8,1,8,128]{3,2,1,0:T(8,128)(2,1)S(1)}, u32[]{:S(2)}, u32[]{:S(2)}) %collective-permute-start.7) | collective-permute-done | bytes 16416 | tf_op jit(solution)/shard_map/ppermute | solution.py:15
  177.6 5.2 %collective-permute-start.8 = (bf16[8,18,1,128]{3,2,1,0:T(2,128)(2,1)S(1)}, bf16[8,18,1,128]{3,2,1,0:T(2,128)(2,1)S(1)}, u32[]{:S(2)}, u32[]{:S(2)}) collective-permute-start(bf16[8,18,1,128]{3,2,1,0:T(2,128)(2,1)S(1)} %get-tuple-element.16), channel_id=1, source_target_pairs={{0,1},{1,2},{2,3},{3,4},{4,5},{5,6},{6,7},{7,8},{8,9},{9,10},{10,1... | collective-permute-start | bytes 110600 | tf_op jit(solution)/shard_map/ppermute | solution.py:14
  182.9 1.9 collective-permute-start.9
  184.9 3.6 %collective-permute-done.9 = bf16[8,18,1,128]{3,2,1,0:T(2,128)(2,1)S(1)} collective-permute-done((bf16[8,18,1,128]{3,2,1,0:T(2,128)(2,1)S(1)}, bf16[8,18,1,128]{3,2,1,0:T(2,128)(2,1)S(1)}, u32[]{:S(2)}, u32[]{:S(2)}) %collective-permute-start.9) | collective-permute-done | bytes 36896 | tf_op jit(solution)/shard_map/ppermute | solution.py:15
  (89 shorter events, 30.5 us)
Async XLA Ops:
  6.5 100.8 %copy-start = (bf16[512,256]{1,0:T(8,128)(2,1)S(1)}, bf16[512,256]{1,0:T(8,128)(2,1)}, u32[]{:S(2)}) copy-start(bf16[512,256]{1,0:T(8,128)(2,1)} %param.10) | copy-start | bytes 786436
  6.5 73.4 %copy-start.2 = (bf16[3,3,3,512,32]{3,4,2,1,0:T(8,128)(2,1)S(1)}, bf16[3,3,3,512,32]{3,4,2,1,0:T(8,128)(2,1)}, u32[]{:S(2)}) copy-start(bf16[3,3,3,512,32]{3,4,2,1,0:T(8,128)(2,1)} %param.7) | copy-start | bytes 2654212
  6.5 64.5 %all-gather.3.cloned.1.call-start = ((), (), s32[]{:S(2)}) async-start(), calls=%async_computation.1 | async-start | bytes 1114112 | tf_op jit(solution)/shard_map/all_gather | solution.py:96
  9.2 143.8 %all-gather.5.cloned.1.call-start = ((), (), s32[]{:S(2)}) async-start(), calls=%async_computation.2 | async-start | bytes 3649536 | tf_op jit(solution)/shard_map/all_gather | solution.py:91
  73.0 11.2 %collective-permute-start = (bf16[8,64,1,512]{3,1,2,0:T(8,128)(2,1)S(1)}, bf16[8,64,1,512]{3,1,2,0:T(8,128)(2,1)S(1)}, u32[]{:S(2)}, u32[]{:S(2)}) collective-permute-start(bf16[8,64,1,512]{3,1,2,0:T(8,128)(2,1)S(1)} %get-tuple-element.8), channel_id=1, source_target_pairs={{0,1},{1,2},{2,3},{3,4},{4,5},{5,6},{6,7},{7,8},{8,9},{9,10},{10,1... | collective-permute-start | bytes 1572872 | tf_op jit(solution)/shard_map/ppermute | solution.py:14
  78.0 10.5 %collective-permute-start.1 = (bf16[8,64,1,512]{3,1,2,0:T(8,128)(2,1)S(1)}, bf16[8,64,1,512]{3,1,2,0:T(8,128)(2,1)S(1)}, u32[]{:S(2)}, u32[]{:S(2)}) collective-permute-start(bf16[8,64,1,512]{3,1,2,0:T(8,128)(2,1)S(1)} %get-tuple-element.9), channel_id=1, source_target_pairs={{1,0},{2,1},{3,2},{4,3},{5,4},{6,5},{7,6},{8,7},{9,8},{10,9},{11,1... | collective-permute-start | bytes 1572872 | tf_op jit(solution)/shard_map/ppermute | solution.py:15
  96.4 10.9 %copy-start.4 = (bf16[8,4,2,512]{3,2,1,0:T(2,128)(2,1)S(1)}, bf16[8,4,2,512]{3,2,1,0:T(2,128)(2,1)}, u32[]{:S(2)}) copy-start(bf16[8,4,2,512]{3,2,1,0:T(2,128)(2,1)} %param.6) | copy-start | bytes 196612
  108.0 5.6 %collective-permute-start.2 = (bf16[8,1,4,256]{3,2,1,0:T(4,128)(2,1)S(1)}, bf16[8,1,4,256]{3,2,1,0:T(4,128)(2,1)S(1)}, u32[]{:S(2)}, u32[]{:S(2)}) collective-permute-start(bf16[8,1,4,256]{3,2,1,0:T(4,128)(2,1)S(1)} %get-tuple-element.23), channel_id=1, source_target_pairs={{0,32},{32,64},{64,96},{96,128},{128,160},{160,192},{192,224},{224... | collective-permute-start | bytes 49160 | tf_op jit(solution)/shard_map/ppermute | solution.py:14
  111.7 6.6 %collective-permute-start.3 = (bf16[8,1,4,256]{3,2,1,0:T(4,128)(2,1)S(1)}, bf16[8,1,4,256]{3,2,1,0:T(4,128)(2,1)S(1)}, u32[]{:S(2)}, u32[]{:S(2)}) collective-permute-start(bf16[8,1,4,256]{3,2,1,0:T(4,128)(2,1)S(1)} %get-tuple-element.22), channel_id=1, source_target_pairs={{32,0},{64,32},{96,64},{128,96},{160,128},{192,160},{224,192},{256... | collective-permute-start | bytes 49160 | tf_op jit(solution)/shard_map/ppermute | solution.py:15
  118.4 7.2 %collective-permute-start.4 = (bf16[8,10,1,256]{3,2,1,0:T(2,128)(2,1)S(1)}, bf16[8,10,1,256]{3,2,1,0:T(2,128)(2,1)S(1)}, u32[]{:S(2)}, u32[]{:S(2)}) collective-permute-start(bf16[8,10,1,256]{3,2,1,0:T(2,128)(2,1)S(1)} %get-tuple-element.20), channel_id=1, source_target_pairs={{0,1},{1,2},{2,3},{3,4},{4,5},{5,6},{6,7},{7,8},{8,9},{9,10},{10,1... | collective-permute-start | bytes 122888 | tf_op jit(solution)/shard_map/ppermute | solution.py:14
  123.1 6.3 %collective-permute-start.5 = (bf16[8,10,1,256]{3,2,1,0:T(2,128)(2,1)S(1)}, bf16[8,10,1,256]{3,2,1,0:T(2,128)(2,1)S(1)}, u32[]{:S(2)}, u32[]{:S(2)}) collective-permute-start(bf16[8,10,1,256]{3,2,1,0:T(2,128)(2,1)S(1)} %get-tuple-element.21), channel_id=1, source_target_pairs={{1,0},{2,1},{3,2},{4,3},{5,4},{6,5},{7,6},{8,7},{9,8},{10,9},{11,1... | collective-permute-start | bytes 122888 | tf_op jit(solution)/shard_map/ppermute | solution.py:15
  161.0 2.4 %copy-start.1 = (bf16[1,3,3,256,256]{4,3,2,1,0:T(8,128)(2,1)S(1)}, bf16[1,3,3,256,256]{4,3,2,1,0:T(8,128)(2,1)}, u32[]{:S(2)}) copy-start(bf16[1,3,3,256,256]{4,3,2,1,0:T(8,128)(2,1)} %copy.50) | copy-start | bytes 3538948
  165.4 2.1 %copy-start.5 = (bf16[256,128]{1,0:T(8,128)(2,1)S(1)}, bf16[256,128]{1,0:T(8,128)(2,1)}, u32[]{:S(2)}) copy-start(bf16[256,128]{1,0:T(8,128)(2,1)} %param.11) | copy-start | bytes 196612
  165.4 19.4 %copy-start.3 = (bf16[3,3,3,128,128]{4,3,2,1,0:T(8,128)(2,1)S(1)}, bf16[3,3,3,128,128]{4,3,2,1,0:T(8,128)(2,1)}, u32[]{:S(2)}) copy-start(bf16[3,3,3,128,128]{4,3,2,1,0:T(8,128)(2,1)} %param.9) | copy-start | bytes 2654212
  168.2 5.3 %collective-permute-start.6 = (bf16[8,1,8,128]{3,2,1,0:T(8,128)(2,1)S(1)}, bf16[8,1,8,128]{3,2,1,0:T(8,128)(2,1)S(1)}, u32[]{:S(2)}, u32[]{:S(2)}) collective-permute-start(bf16[8,1,8,128]{3,2,1,0:T(8,128)(2,1)S(1)} %get-tuple-element.18), channel_id=1, source_target_pairs={{0,32},{32,64},{64,96},{96,128},{128,160},{160,192},{192,224},{224... | collective-permute-start | bytes 49160 | tf_op jit(solution)/shard_map/ppermute | solution.py:14
  170.9 6.6 %collective-permute-start.7 = (bf16[8,1,8,128]{3,2,1,0:T(8,128)(2,1)S(1)}, bf16[8,1,8,128]{3,2,1,0:T(8,128)(2,1)S(1)}, u32[]{:S(2)}, u32[]{:S(2)}) collective-permute-start(bf16[8,1,8,128]{3,2,1,0:T(8,128)(2,1)S(1)} %get-tuple-element.19), channel_id=1, source_target_pairs={{32,0},{64,32},{96,64},{128,96},{160,128},{192,160},{224,192},{256... | collective-permute-start | bytes 49160 | tf_op jit(solution)/shard_map/ppermute | solution.py:15
  177.6 7.3 %collective-permute-start.8 = (bf16[8,18,1,128]{3,2,1,0:T(2,128)(2,1)S(1)}, bf16[8,18,1,128]{3,2,1,0:T(2,128)(2,1)S(1)}, u32[]{:S(2)}, u32[]{:S(2)}) collective-permute-start(bf16[8,18,1,128]{3,2,1,0:T(2,128)(2,1)S(1)} %get-tuple-element.16), channel_id=1, source_target_pairs={{0,1},{1,2},{2,3},{3,4},{4,5},{5,6},{6,7},{7,8},{8,9},{9,10},{10,1... | collective-permute-start | bytes 110600 | tf_op jit(solution)/shard_map/ppermute | solution.py:14
  182.9 5.7 %collective-permute-start.9 = (bf16[8,18,1,128]{3,2,1,0:T(2,128)(2,1)S(1)}, bf16[8,18,1,128]{3,2,1,0:T(2,128)(2,1)S(1)}, u32[]{:S(2)}, u32[]{:S(2)}) collective-permute-start(bf16[8,18,1,128]{3,2,1,0:T(2,128)(2,1)S(1)} %get-tuple-element.17), channel_id=1, source_target_pairs={{1,0},{2,1},{3,2},{4,3},{5,4},{6,5},{7,6},{8,7},{9,8},{10,9},{11,1... | collective-permute-start | bytes 110600 | tf_op jit(solution)/shard_map/ppermute | solution.py:15
Sparse Core Ops, SparseCore 0:
  10.4 60.6 all-gather.2
  73.1 79.7 all-gather.4
where the time goes:
time: 201 us; the launch traced here: 200 us
  waiting for transfers between devices  102 us (51%)
  starting transfers between devices  31.8 us (16%)
  local copies, waits for them, and re-layouts  20.9 us (10%)
  matrix products  14.4 us (7%)
  between operations  13.9 us (7%)
  blocking collectives  9.77 us (5%)
  other arithmetic  7.18 us (4%)
    all_gather x1, waiting for transfers between devices, body(): whole = lax.all_gather(first_act, 'grp', axis=1, tiled=True)  61.1 us
    ppermute x5, starting transfers between devices, with_halo(): before = lax.ppermute(last, axis, up)  21.3 us
    ppermute x5, waiting for transfers between devices, with_halo(): after = lax.ppermute(initial, axis, down)  20.3 us
    all_gather x1, waiting for transfers between devices, middle_conv(): lax.all_gather(mid_filters, 'tile', axis=4, tiled=True)  16.2 us
    unnamed x35, local copies, waits for them, and re-layouts  12.7 us
    ppermute x5, starting transfers between devices, with_halo(): after = lax.ppermute(initial, axis, down)  10.5 us
    all_to_all x1, blocking collectives, body(): lax.all_to_all(filtered, 'grp', split_axis=1, concat_axis=3, tiled=True)  9.77 us
    dot_general x4, matrix products, apply_columns(): jnp.dot(columns[frame_step:frame_step + frames], folded[frame_step], pref...  6.33 us
  transfers between devices with their start and end apart: 12, of which 8 were waited for; matrix products, arithmetic and copies ran while one was open for 10% of the time, Pallas kernels for 0%

commit v1 on v0

--- a/solution.py
+++ b/solution.py
@@ -88,7 +88,13 @@
 
 def middle_conv(extended, mid_filters):
     columns = stencil_columns(extended)
-    return apply_columns(columns, lax.all_gather(mid_filters, "tile", axis=4, tiled=True))
+
+    def wrap_types(x_in):
+        return jnp.concatenate(
+            jax.lax.all_to_all(jnp.stack(jax.lax.axis_size("tile") * [x_in]), "tile", 0, 0), axis=4
+        )
+
+    return apply_columns(columns, wrap_types(mid_filters))
 
 
 def body(latent, coarse_filters, mid_filters, fine_filters, coarse_proj, mid_proj):

time: 201 us -> 323 us (1.61)
  waiting for transfers between devices: 102 us -> 220 us
  starting transfers between devices: 31.8 us -> 50.6 us
  local copies, waits for them, and re-layouts: 20.9 us -> 11 us
  matrix products: 14.4 us -> 10.2 us
    ppermute x5, waiting for transfers between devices: 4.11 us -> 132 us  [with_halo(): before = lax.ppermute(last, axis, up)]
    all_gather x1 -> x0, waiting for transfers between devices: 16.2 us -> none  [middle_conv(): lax.all_gather(mid_filters, 'tile', axis=4, tiled=True)]
    all_to_all x0 -> x1, starting transfers between devices: none -> 13.8 us  [wrap_types(): jax.lax.all_to_all(jnp.stack(jax.lax.axis_size('tile') * [x_in]), 'tile',...]
    unnamed x35 -> x32, local copies, waits for them, and re-layouts: 12.7 us -> 2.52 us
    ppermute x5, starting transfers between devices: 21.3 us -> 27 us  [with_halo(): before = lax.ppermute(last, axis, up)]
    ppermute x5, waiting for transfers between devices: 20.3 us -> 25.3 us  [with_halo(): after = lax.ppermute(initial, axis, down)]
  transfers between devices with their start and end apart: 12 -> 12, of which waited for: 8 -> 9; matrix products, arithmetic and copies ran while one was open for 10% -> 1% of each run, Pallas kernels for 0% -> 0%
where the time goes in v1:
time: 323 us
  waiting for transfers between devices  220 us (68%)
  starting transfers between devices  50.6 us (16%)
  between operations  13.9 us (4%)
  local copies, waits for them, and re-layouts  11 us (3%)
  matrix products  10.2 us (3%)
  blocking collectives  9.77 us (3%)
  other arithmetic  7.17 us (2%)
    ppermute x5, waiting for transfers between devices, with_halo(): before = lax.ppermute(last, axis, up)  132 us
    all_gather x1, waiting for transfers between devices, body(): whole = lax.all_gather(first_act, 'grp', axis=1, tiled=True)  61.9 us
    ppermute x5, starting transfers between devices, with_halo(): before = lax.ppermute(last, axis, up)  27 us
    ppermute x5, waiting for transfers between devices, with_halo(): after = lax.ppermute(initial, axis, down)  25.3 us
    all_to_all x1, starting transfers between devices, wrap_types(): jax.lax.all_to_all(jnp.stack(jax.lax.axis_size('tile') * [x_in]), 'tile',...  13.8 us
    ppermute x5, starting transfers between devices, with_halo(): after = lax.ppermute(initial, axis, down)  9.78 us
    all_to_all x1, blocking collectives, body(): lax.all_to_all(filtered, 'grp', split_axis=1, concat_axis=3, tiled=True)  9.77 us
  transfers between devices with their start and end apart: 12, of which 9 were waited for; matrix products, arithmetic and copies ran while one was open for 1% of the time, Pallas kernels for 0%

profile of v1, /device:TPU:7, one launch (start us, length us, event | category | flops | bytes accessed | tf_op | source)
XLA Modules:
  0.0 322.7 jit_solution(10591971579450849039)
XLA Ops:
  9.2 61.9 %all-gather.2.cloned.1.call-done = bf16[8,64,2,512]{3,0,2,1:T(8,128)(2,1)} async-done(((bf16[8,4,2,512]{3,0,2,1:T(8,128)(2,1)}), bf16[8,64,2,512]{3,0,2,1:T(8,128)(2,1)}) %all-gather.2.cloned.1.call-update) | async-done | bytes 1048592 | tf_op jit(solution)/shard_map/all_gather | solution.py:102
  71.1 1.8 copy.26
  73.0 5.1 %collective-permute-start = (bf16[8,64,1,512]{3,1,2,0:T(8,128)(2,1)S(1)}, bf16[8,64,1,512]{3,1,2,0:T(8,128)(2,1)S(1)}, u32[]{:S(2)}, u32[]{:S(2)}) collective-permute-start(bf16[8,64,1,512]{3,1,2,0:T(8,128)(2,1)S(1)} %get-tuple-element.8), channel_id=1, source_target_pairs={{0,1},{1,2},{2,3},{3,4},{4,5},{5,6},{6,7},{7,8},{8,9},{9,10},{10,1... | collective-permute-start | bytes 1572872 | tf_op jit(solution)/shard_map/ppermute | solution.py:14
  78.0 1.9 collective-permute-start.1
  80.0 4.1 %collective-permute-done = bf16[8,64,1,512]{3,1,2,0:T(8,128)(2,1)S(1)} collective-permute-done((bf16[8,64,1,512]{3,1,2,0:T(8,128)(2,1)S(1)}, bf16[8,64,1,512]{3,1,2,0:T(8,128)(2,1)S(1)}, u32[]{:S(2)}, u32[]{:S(2)}) %collective-permute-start) | collective-permute-done | bytes 524320 | tf_op jit(solution)/shard_map/ppermute | solution.py:14
  84.1 4.4 %collective-permute-done.1 = bf16[8,64,1,512]{3,1,2,0:T(8,128)(2,1)S(1)} collective-permute-done((bf16[8,64,1,512]{3,1,2,0:T(8,128)(2,1)S(1)}, bf16[8,64,1,512]{3,1,2,0:T(8,128)(2,1)S(1)}, u32[]{:S(2)}, u32[]{:S(2)}) %collective-permute-start.1) | collective-permute-done | bytes 524320 | tf_op jit(solution)/shard_map/ppermute | solution.py:15
  93.9 2.5 fusion.24
  97.0 9.8 %all_to_all.14 = bf16[16,2,1024]{2,1,0:T(2,128)(2,1)S(1)} all-to-all(bf16[16,2,1024]{2,1,0:T(2,128)(2,1)S(1)} %reshape.96), channel_id=1, replica_groups=mesh['grp'=16,'tile'=32] {'grp'}, dimensions={0} | all-to-all | bytes 131072 | tf_op jit(solution)/shard_map/all_to_all | solution.py:106
  106.8 2.0 stack.2
  108.8 13.8 %all-to-all-start.1 = ((bf16[32,3,3,3,256,8]{4,5,3,2,1,0:T(8,128)(2,1)}), bf16[32,3,3,3,256,8]{4,5,3,2,1,0:T(8,128)(2,1)}, u32[]{:S(2)}, u32[]{:S(2)}) async-start(bf16[32,3,3,3,256,8]{4,5,3,2,1,0:T(8,128)(2,1)} %stack.2), calls=%async_computation.1 | async-start | bytes 7077888 | tf_op jit(solution)/shard_map/all_to_all | solution.py:94
  123.9 3.7 %collective-permute-start.2 = (bf16[8,1,4,256]{3,2,1,0:T(4,128)(2,1)S(1)}, bf16[8,1,4,256]{3,2,1,0:T(4,128)(2,1)S(1)}, u32[]{:S(2)}, u32[]{:S(2)}) collective-permute-start(bf16[8,1,4,256]{3,2,1,0:T(4,128)(2,1)S(1)} %get-tuple-element.23), channel_id=1, source_target_pairs={{0,32},{32,64},{64,96},{96,128},{128,160},{160,192},{192,224},{224... | collective-permute-start | bytes 49160 | tf_op jit(solution)/shard_map/ppermute | solution.py:14
  127.5 1.9 collective-permute-start.3
  129.6 5.0 %collective-permute-done.3 = bf16[8,1,4,256]{3,2,1,0:T(4,128)(2,1)S(1)} collective-permute-done((bf16[8,1,4,256]{3,2,1,0:T(4,128)(2,1)S(1)}, bf16[8,1,4,256]{3,2,1,0:T(4,128)(2,1)S(1)}, u32[]{:S(2)}, u32[]{:S(2)}) %collective-permute-start.3) | collective-permute-done | bytes 16416 | tf_op jit(solution)/shard_map/ppermute | solution.py:15
  134.7 4.6 %collective-permute-start.4 = (bf16[8,10,1,256]{3,2,1,0:T(2,128)(2,1)S(1)}, bf16[8,10,1,256]{3,2,1,0:T(2,128)(2,1)S(1)}, u32[]{:S(2)}, u32[]{:S(2)}) collective-permute-start(bf16[8,10,1,256]{3,2,1,0:T(2,128)(2,1)S(1)} %get-tuple-element.20), channel_id=1, source_target_pairs={{0,1},{1,2},{2,3},{3,4},{4,5},{5,6},{6,7},{7,8},{8,9},{9,10},{10,1... | collective-permute-start | bytes 122888 | tf_op jit(solution)/shard_map/ppermute | solution.py:14
  139.3 2.1 collective-permute-start.5
  141.8 127.7 %collective-permute-done.4 = bf16[8,10,1,256]{3,2,1,0:T(2,128)(2,1)S(1)} collective-permute-done((bf16[8,10,1,256]{3,2,1,0:T(2,128)(2,1)S(1)}, bf16[8,10,1,256]{3,2,1,0:T(2,128)(2,1)S(1)}, u32[]{:S(2)}, u32[]{:S(2)}) %collective-permute-start.4) | collective-permute-done | bytes 40992 | tf_op jit(solution)/shard_map/ppermute | solution.py:14
  269.5 7.7 %collective-permute-done.5 = bf16[8,10,1,256]{3,2,1,0:T(2,128)(2,1)S(1)} collective-permute-done((bf16[8,10,1,256]{3,2,1,0:T(2,128)(2,1)S(1)}, bf16[8,10,1,256]{3,2,1,0:T(2,128)(2,1)S(1)}, u32[]{:S(2)}, u32[]{:S(2)}) %collective-permute-start.5) | collective-permute-done | bytes 40992 | tf_op jit(solution)/shard_map/ppermute | solution.py:15
  279.5 2.2 fusion.40
  284.8 3.7 %collective-permute-start.6 = (bf16[8,1,8,128]{3,2,1,0:T(8,128)(2,1)S(1)}, bf16[8,1,8,128]{3,2,1,0:T(8,128)(2,1)S(1)}, u32[]{:S(2)}, u32[]{:S(2)}) collective-permute-start(bf16[8,1,8,128]{3,2,1,0:T(8,128)(2,1)S(1)} %get-tuple-element.18), channel_id=1, source_target_pairs={{0,32},{32,64},{64,96},{96,128},{128,160},{160,192},{192,224},{224... | collective-permute-start | bytes 49160 | tf_op jit(solution)/shard_map/ppermute | solution.py:14
  288.5 1.9 collective-permute-start.7
  290.4 4.7 %collective-permute-done.7 = bf16[8,1,8,128]{3,2,1,0:T(8,128)(2,1)S(1)} collective-permute-done((bf16[8,1,8,128]{3,2,1,0:T(8,128)(2,1)S(1)}, bf16[8,1,8,128]{3,2,1,0:T(8,128)(2,1)S(1)}, u32[]{:S(2)}, u32[]{:S(2)}) %collective-permute-start.7) | collective-permute-done | bytes 16416 | tf_op jit(solution)/shard_map/ppermute | solution.py:15
  295.2 10.0 %collective-permute-start.8 = (bf16[8,18,1,128]{3,2,1,0:T(2,128)(2,1)S(1)}, bf16[8,18,1,128]{3,2,1,0:T(2,128)(2,1)S(1)}, u32[]{:S(2)}, u32[]{:S(2)}) collective-permute-start(bf16[8,18,1,128]{3,2,1,0:T(2,128)(2,1)S(1)} %get-tuple-element.16), channel_id=1, source_target_pairs={{0,1},{1,2},{2,3},{3,4},{4,5},{5,6},{6,7},{7,8},{8,9},{9,10},{10,1... | collective-permute-start | bytes 110600 | tf_op jit(solution)/shard_map/ppermute | solution.py:14
  305.2 1.9 collective-permute-start.9
  307.3 3.6 %collective-permute-done.9 = bf16[8,18,1,128]{3,2,1,0:T(2,128)(2,1)S(1)} collective-permute-done((bf16[8,18,1,128]{3,2,1,0:T(2,128)(2,1)S(1)}, bf16[8,18,1,128]{3,2,1,0:T(2,128)(2,1)S(1)}, u32[]{:S(2)}, u32[]{:S(2)}) %collective-permute-start.9) | collective-permute-done | bytes 36896 | tf_op jit(solution)/shard_map/ppermute | solution.py:15
  (86 shorter events, 20.8 us)
Async XLA Ops:
  6.5 116.7 %copy-start = (bf16[512,256]{1,0:T(8,128)(2,1)S(1)}, bf16[512,256]{1,0:T(8,128)(2,1)}, u32[]{:S(2)}) copy-start(bf16[512,256]{1,0:T(8,128)(2,1)} %param.10) | copy-start | bytes 786436
  6.5 73.4 %copy-start.1 = (bf16[3,3,3,512,32]{3,4,2,1,0:T(8,128)(2,1)S(1)}, bf16[3,3,3,512,32]{3,4,2,1,0:T(8,128)(2,1)}, u32[]{:S(2)}) copy-start(bf16[3,3,3,512,32]{3,4,2,1,0:T(8,128)(2,1)} %param.7) | copy-start | bytes 2654212
  6.5 64.5 %all-gather.2.cloned.1.call-start = ((), (), s32[]{:S(2)}) async-start(), calls=%async_computation.2 | async-start | bytes 1114112 | tf_op jit(solution)/shard_map/all_gather | solution.py:102
  73.0 11.2 %collective-permute-start = (bf16[8,64,1,512]{3,1,2,0:T(8,128)(2,1)S(1)}, bf16[8,64,1,512]{3,1,2,0:T(8,128)(2,1)S(1)}, u32[]{:S(2)}, u32[]{:S(2)}) collective-permute-start(bf16[8,64,1,512]{3,1,2,0:T(8,128)(2,1)S(1)} %get-tuple-element.8), channel_id=1, source_target_pairs={{0,1},{1,2},{2,3},{3,4},{4,5},{5,6},{6,7},{7,8},{8,9},{9,10},{10,1... | collective-permute-start | bytes 1572872 | tf_op jit(solution)/shard_map/ppermute | solution.py:14
  78.0 10.5 %collective-permute-start.1 = (bf16[8,64,1,512]{3,1,2,0:T(8,128)(2,1)S(1)}, bf16[8,64,1,512]{3,1,2,0:T(8,128)(2,1)S(1)}, u32[]{:S(2)}, u32[]{:S(2)}) collective-permute-start(bf16[8,64,1,512]{3,1,2,0:T(8,128)(2,1)S(1)} %get-tuple-element.9), channel_id=1, source_target_pairs={{1,0},{2,1},{3,2},{4,3},{5,4},{6,5},{7,6},{8,7},{9,8},{10,9},{11,1... | collective-permute-start | bytes 1572872 | tf_op jit(solution)/shard_map/ppermute | solution.py:15
  93.9 12.8 %copy-start.4 = (bf16[3,3,3,256,8]{3,4,2,1,0:T(8,128)(2,1)S(1)}, bf16[3,3,3,256,8]{3,4,2,1,0:T(8,128)(2,1)}, u32[]{:S(2)}) copy-start(bf16[3,3,3,256,8]{3,4,2,1,0:T(8,128)(2,1)} %param.8) | copy-start | bytes 331780
  108.8 14.4 %copy-start.3 = (bf16[8,4,2,512]{3,2,1,0:T(2,128)(2,1)S(1)}, bf16[8,4,2,512]{3,2,1,0:T(2,128)(2,1)}, u32[]{:S(2)}) copy-start(bf16[8,4,2,512]{3,2,1,0:T(2,128)(2,1)} %param.6) | copy-start | bytes 196612
  108.8 170.7 %all-to-all-start.1 = ((bf16[32,3,3,3,256,8]{4,5,3,2,1,0:T(8,128)(2,1)}), bf16[32,3,3,3,256,8]{4,5,3,2,1,0:T(8,128)(2,1)}, u32[]{:S(2)}, u32[]{:S(2)}) async-start(bf16[32,3,3,3,256,8]{4,5,3,2,1,0:T(8,128)(2,1)} %stack.2), calls=%async_computation.1 | async-start | bytes 7077888 | tf_op jit(solution)/shard_map/all_to_all | solution.py:94
  123.9 5.6 %collective-permute-start.2 = (bf16[8,1,4,256]{3,2,1,0:T(4,128)(2,1)S(1)}, bf16[8,1,4,256]{3,2,1,0:T(4,128)(2,1)S(1)}, u32[]{:S(2)}, u32[]{:S(2)}) collective-permute-start(bf16[8,1,4,256]{3,2,1,0:T(4,128)(2,1)S(1)} %get-tuple-element.23), channel_id=1, source_target_pairs={{0,32},{32,64},{64,96},{96,128},{128,160},{160,192},{192,224},{224... | collective-permute-start | bytes 49160 | tf_op jit(solution)/shard_map/ppermute | solution.py:14
  127.5 7.0 %collective-permute-start.3 = (bf16[8,1,4,256]{3,2,1,0:T(4,128)(2,1)S(1)}, bf16[8,1,4,256]{3,2,1,0:T(4,128)(2,1)S(1)}, u32[]{:S(2)}, u32[]{:S(2)}) collective-permute-start(bf16[8,1,4,256]{3,2,1,0:T(4,128)(2,1)S(1)} %get-tuple-element.22), channel_id=1, source_target_pairs={{32,0},{64,32},{96,64},{128,96},{160,128},{192,160},{224,192},{256... | collective-permute-start | bytes 49160 | tf_op jit(solution)/shard_map/ppermute | solution.py:15
  134.7 134.8 %collective-permute-start.4 = (bf16[8,10,1,256]{3,2,1,0:T(2,128)(2,1)S(1)}, bf16[8,10,1,256]{3,2,1,0:T(2,128)(2,1)S(1)}, u32[]{:S(2)}, u32[]{:S(2)}) collective-permute-start(bf16[8,10,1,256]{3,2,1,0:T(2,128)(2,1)S(1)} %get-tuple-element.20), channel_id=1, source_target_pairs={{0,1},{1,2},{2,3},{3,4},{4,5},{5,6},{6,7},{7,8},{8,9},{9,10},{10,1... | collective-permute-start | bytes 122888 | tf_op jit(solution)/shard_map/ppermute | solution.py:14
  139.3 138.0 %collective-permute-start.5 = (bf16[8,10,1,256]{3,2,1,0:T(2,128)(2,1)S(1)}, bf16[8,10,1,256]{3,2,1,0:T(2,128)(2,1)S(1)}, u32[]{:S(2)}, u32[]{:S(2)}) collective-permute-start(bf16[8,10,1,256]{3,2,1,0:T(2,128)(2,1)S(1)} %get-tuple-element.21), channel_id=1, source_target_pairs={{1,0},{2,1},{3,2},{4,3},{5,4},{6,5},{7,6},{8,7},{9,8},{10,9},{11,1... | collective-permute-start | bytes 122888 | tf_op jit(solution)/shard_map/ppermute | solution.py:15
  283.2 0.8 copy-start.5
  284.1 23.1 %copy-start.2 = (bf16[3,3,3,128,128]{4,3,2,1,0:T(8,128)(2,1)S(1)}, bf16[3,3,3,128,128]{4,3,2,1,0:T(8,128)(2,1)}, u32[]{:S(2)}) copy-start(bf16[3,3,3,128,128]{4,3,2,1,0:T(8,128)(2,1)} %param.9) | copy-start | bytes 2654212
  284.8 5.6 %collective-permute-start.6 = (bf16[8,1,8,128]{3,2,1,0:T(8,128)(2,1)S(1)}, bf16[8,1,8,128]{3,2,1,0:T(8,128)(2,1)S(1)}, u32[]{:S(2)}, u32[]{:S(2)}) collective-permute-start(bf16[8,1,8,128]{3,2,1,0:T(8,128)(2,1)S(1)} %get-tuple-element.18), channel_id=1, source_target_pairs={{0,32},{32,64},{64,96},{96,128},{128,160},{160,192},{192,224},{224... | collective-permute-start | bytes 49160 | tf_op jit(solution)/shard_map/ppermute | solution.py:14
  288.5 6.6 %collective-permute-start.7 = (bf16[8,1,8,128]{3,2,1,0:T(8,128)(2,1)S(1)}, bf16[8,1,8,128]{3,2,1,0:T(8,128)(2,1)S(1)}, u32[]{:S(2)}, u32[]{:S(2)}) collective-permute-start(bf16[8,1,8,128]{3,2,1,0:T(8,128)(2,1)S(1)} %get-tuple-element.19), channel_id=1, source_target_pairs={{32,0},{64,32},{96,64},{128,96},{160,128},{192,160},{224,192},{256... | collective-permute-start | bytes 49160 | tf_op jit(solution)/shard_map/ppermute | solution.py:15
  295.2 12.1 %collective-permute-start.8 = (bf16[8,18,1,128]{3,2,1,0:T(2,128)(2,1)S(1)}, bf16[8,18,1,128]{3,2,1,0:T(2,128)(2,1)S(1)}, u32[]{:S(2)}, u32[]{:S(2)}) collective-permute-start(bf16[8,18,1,128]{3,2,1,0:T(2,128)(2,1)S(1)} %get-tuple-element.16), channel_id=1, source_target_pairs={{0,1},{1,2},{2,3},{3,4},{4,5},{5,6},{6,7},{7,8},{8,9},{9,10},{10,1... | collective-permute-start | bytes 110600 | tf_op jit(solution)/shard_map/ppermute | solution.py:14
  305.2 5.7 %collective-permute-start.9 = (bf16[8,18,1,128]{3,2,1,0:T(2,128)(2,1)S(1)}, bf16[8,18,1,128]{3,2,1,0:T(2,128)(2,1)S(1)}, u32[]{:S(2)}, u32[]{:S(2)}) collective-permute-start(bf16[8,18,1,128]{3,2,1,0:T(2,128)(2,1)S(1)} %get-tuple-element.17), channel_id=1, source_target_pairs={{1,0},{2,1},{3,2},{4,3},{5,4},{6,5},{7,6},{8,7},{9,8},{10,9},{11,1... | collective-permute-start | bytes 110600 | tf_op jit(solution)/shard_map/ppermute | solution.py:15
Sparse Core Ops, SparseCore 0:
  10.4 60.6 all-gather.1
